TPU v7x, 32 devices: a whole 2x2x4 slice. The times are simulated.
32 devices in a mesh: trade: 4 (over z), path: 8 (over y, x, core).
Axes of the slice: x: 2, y: 2, z: 4, core: 2. Of those that a mesh axis runs over, the one named last changes fastest.
Arguments:
- start_state: float32 [4096, 32], P('path'), may hold values from -6 to 6
- shocks: float32 [2, 4096, 32], P(None, 'path'), may hold values from -6 to 6
- loadings: float32 [32, 32768], P(None, 'trade'), may hold values from -1 to 1
- strikes: float32 [32768], P('trade'), may hold values from -0.5 to 1
- notionals: float32 [32768], P('trade'), may hold values from -1 to 1
- trade_set: int32 [32768], P('trade'), may hold values from 0 to 1023
- live_counts: int32 [4], replicated, may hold values from 1 to 8192, 24576 in all
- weights: int32 [4096], P('path'), may hold values from 1 to 16
- thresholds: int32 [1024], P('trade'), may hold values from 0 to 8
Outputs:
- exposure: float32 [2, 1024, 4096], P(None, 'trade', 'path')
- expected: float32 [2, 1024], P(None, 'trade')
Inputs may be any that keep to these rules, and one draw needn't show every extreme that they name: The live slots of group g are its first live_counts[g] slots; the counts sum to 24576 and some group is full.
All inputs are finite; a program needn't handle non-finite values.
Results may differ from a plain program's by a relative error of at most 0.0003.
Values sent between devices are 32-bit elements; how exact they have to be, the bound alone decides.
No kernel may reach another device: no remote copies, remote signals or barrier semaphores. Data moves between devices by JAX's collectives and lax.ppermute only.
A program may use at most 128 MiB of HBM per device.

v0:
```python
import functools

import jax
import jax.numpy as jnp
from jax import lax
from jax.experimental import pallas as pl
from jax.experimental.pallas import tpu as pltpu
from jax.sharding import PartitionSpec as P

HIGHEST_PREC = lax.Precision.HIGHEST
ROOT_HALF = 0.7071067811865476
F32 = jnp.float32
BF16 = jnp.bfloat16
TILE = 512
DEPTH = 256
VMEM_BYTES = 56 * 1024 * 1024
NN = (((1,), (0,)), ((), ()))
NT = (((1,), (1,)), ((), ()))


def mm(a, b, dims=NN):
    return lax.dot_general(a, b, dims, preferred_element_type=F32)


def mm_full(a, b, dims=NN):
    return lax.dot_general(a, b, dims, preferred_element_type=F32, precision=HIGHEST_PREC)


def split2(x):
    hi = x.astype(BF16)
    return hi, (x - hi.astype(F32)).astype(BF16)


def split3(x):
    hi = x.astype(BF16)
    rest = x - hi.astype(F32)
    mid = rest.astype(BF16)
    return hi, mid, (rest - mid.astype(F32)).astype(BF16)


def basis_rows(state):
    return jnp.concatenate([state, (state * state - 1.0) * ROOT_HALF], axis=0)


def moment_kernel(
    counts_ref, start_ref, shocks_ref, weights_ref, load_ref, strike_ref, notional_ref, set_ref,
    net_ref, states_scr, wide_scr, load_scr,
):
    factors, paths = start_ref.shape
    dates = shocks_ref.shape[0]
    slots = load_ref.shape[1]
    sets = net_ref.shape[0]
    filled = counts_ref[lax.axis_index("trade")]

    weight_row = weights_ref[...].astype(F32)
    state = start_ref[...]
    ones = jnp.where(lax.broadcasted_iota(jnp.int32, (DEPTH - 6 * factors, paths), 0) < 3, 1.0, 0.0)
    for date in range(dates):
        hi, lo = split2(basis_rows(state) * weight_row)
        wide_scr[date] = jnp.concatenate([hi, lo], axis=0)
        state = 0.8 * state + 0.6 * shocks_ref[date]
        hi, mid, low = split3(state)
        hi, mid, low = hi.astype(F32), mid.astype(F32), low.astype(F32)
        stacked = jnp.concatenate([hi, hi, mid, mid, hi, low, ones], axis=0)
        states_scr[pl.ds(date * paths, paths), :] = stacked.T.astype(BF16)
    net_ref[...] = jnp.zeros_like(net_ref)
    load_scr[...] = jnp.zeros_like(load_scr)

    def step(index, carry):
        cols = pl.ds(pl.multiple_of(index * TILE, TILE), TILE)
        hi, mid, low = split3(load_ref[:, cols])
        for part, piece in enumerate((hi, mid, hi, mid, low, hi)):
            load_scr[pl.ds(part * factors, factors), :] = piece
        s_hi, s_mid, s_low = split3(-strike_ref[:, cols])
        rows = lax.broadcasted_iota(jnp.int32, (16, TILE), 0)
        strike_rows = jnp.where(
            rows == 0, s_hi.astype(F32), jnp.where(rows == 1, s_mid.astype(F32), jnp.where(rows == 2, s_low.astype(F32), 0.0))
        )
        load_scr[pl.ds(6 * factors, 16), :] = strike_rows.astype(BF16)
        slot_ids = index * TILE + lax.broadcasted_iota(jnp.int32, (1, TILE), 1)
        scaled = jnp.where(slot_ids < filled, notional_ref[:, cols], 0.0)
        his, los = [], []
        for date in range(dates):
            pay = mm(states_scr[pl.ds(date * paths, paths), :], load_scr[...])
            hi, lo = split2(jnp.maximum(pay, 0.0))
            wide = 2 * factors
            both = mm(wide_scr[date], hi)
            moment = both[:wide] + both[wide:] + mm(wide_scr[date, :wide], lo)
            hi, lo = split2(moment * scaled)
            his.append(hi)
            los.append(lo)
        stacked = jnp.concatenate(his + los, axis=0)
        one_hot = jnp.where(
            lax.broadcasted_iota(jnp.int32, (sets, TILE), 0) == set_ref[:, cols], 1.0, 0.0
        ).astype(BF16)
        summed = mm(one_hot, stacked, NT)
        half = summed.shape[1] // 2
        net_ref[...] += summed[:, :half] + summed[:, half:]
        return carry

    lax.fori_loop(0, slots // TILE, step, 0)


def inverse_kernel(start_ref, shock_ref, weights_ref, inverse_ref):
    blocks, factors, _ = start_ref.shape
    dates = inverse_ref.shape[0]
    wide = 2 * factors
    sub = lax.broadcasted_iota(jnp.int32, (wide, wide), 0)
    lane = lax.broadcasted_iota(jnp.int32, (wide, wide), 1)

    def step(block, grams):
        weight_row = weights_ref[block].astype(F32)
        state = start_ref[block]
        results = []
        for date in range(dates):
            if date > 0:
                state = 0.8 * state + 0.6 * shock_ref[date - 1, block]
            basis = basis_rows(state)
            results.append(grams[date] + mm_full(basis * weight_row, basis, NT))
        return tuple(results)

    grams = lax.fori_loop(0, blocks, step, tuple(jnp.zeros((wide, wide), F32) for _ in range(dates)))
    work = list(grams)
    for k in range(wide):
        for date in range(dates):
            mat = work[date]
            row = mat[k : k + 1, :]
            col = mat[:, k : k + 1]
            pivot = 1.0 / mat[k : k + 1, k : k + 1]
            row = jnp.where(lane[:1] == k, 1.0, row) * pivot
            work[date] = jnp.where(sub == k, row, jnp.where(lane == k, 0.0, mat) - col * row)
    eye = jnp.where(sub == lane, 1.0, 0.0)
    for date in range(dates):
        approx = work[date]
        inverse_ref[date] = approx + mm_full(approx, eye - mm_full(grams[date], approx))


def exposure_kernel(
    totals_ref, inverse_ref, start_ref, shock_ref, weights_ref, limits_ref, exposure_ref, expected_ref
):
    blocks, factors, paths = start_ref.shape
    dates = inverse_ref.shape[0]
    wide = 2 * factors
    mine = lax.axis_index("path")
    limits = 0.25 * limits_ref[...].astype(F32)
    coeffs = []
    for date in range(dates):
        hi, lo = split2(mm_full(totals_ref[:, date * wide : (date + 1) * wide], inverse_ref[date]))
        coeffs.append(jnp.concatenate([hi, hi, lo], axis=1))

    def netted(block):
        state = start_ref[block]
        results = []
        for date in range(dates):
            if date > 0:
                state = 0.8 * state + 0.6 * shock_ref[date - 1, block]
            hi, lo = split2(basis_rows(state))
            value = mm(coeffs[date], jnp.concatenate([hi, lo, hi], axis=0))
            results.append(jnp.maximum(value - limits, 0.0))
        return results

    own = netted(mine)
    for date in range(dates):
        exposure_ref[date] = own[date]

    def step(block, carry):
        weight_row = weights_ref[block].astype(F32)
        sums, total = carry
        results = []
        parts = netted(block)
        for date in range(dates):
            product = parts[date] * weight_row
            partial = sums[date]
            for c in range(paths // 128):
                partial = partial + product[:, c * 128 : (c + 1) * 128]
            results.append(partial)
        return (tuple(results), total + jnp.sum(weight_row, keepdims=True))

    sets = limits.shape[0]
    sums, total = lax.fori_loop(
        0, blocks, step,
        (tuple(jnp.zeros((sets, 128), F32) for _ in range(dates)), jnp.zeros((1, 1), F32)),
    )
    for date in range(dates):
        expected_ref[date : date + 1, :] = jnp.sum(sums[date].T, axis=0, keepdims=True) / total


def body(
    start_state, shocks, loadings, strikes, notionals, trade_set, live_counts, weights, thresholds
):
    paths, factors = start_state.shape
    dates = shocks.shape[0]
    slots = loadings.shape[1]
    owned = thresholds.shape[0]
    groups = lax.axis_size("trade")
    ranks = lax.axis_size("path")
    sets = owned * groups
    wide = 2 * factors

    start_t = start_state.T
    shocks_t = jnp.swapaxes(shocks, 1, 2)
    weights_row = weights[None, :]
    vmem = pl.BlockSpec(memory_space=pltpu.VMEM)
    smem = pl.BlockSpec(memory_space=pltpu.SMEM)
    params = pltpu.CompilerParams(vmem_limit_bytes=VMEM_BYTES)

    all_start = lax.all_gather(start_t, "path")
    all_shocks = [lax.all_gather(shocks_t[date], "path") for date in range(dates - 1)]
    all_shocks = jnp.stack(all_shocks) if len(all_shocks) > 1 else all_shocks[0][None]
    all_weights = lax.all_gather(weights_row, "path")

    net = pl.pallas_call(
        moment_kernel,
        out_shape=jax.ShapeDtypeStruct((sets, dates * wide), F32),
        in_specs=[smem] + [vmem] * 7,
        out_specs=vmem,
        scratch_shapes=[
            pltpu.VMEM((dates * paths, DEPTH), BF16),
            pltpu.VMEM((dates, 2 * wide, paths), BF16),
            pltpu.VMEM((DEPTH, TILE), BF16),
        ],
        compiler_params=params,
        cost_estimate=pl.CostEstimate(flops=16 * 10**9, bytes_accessed=4 * 10**6, transcendentals=0),
        name="net_moments",
    )(
        live_counts, start_t, shocks_t, weights_row, loadings, strikes[None, :], notionals[None, :],
        trade_set[None, :],
    )
    share = lax.psum_scatter(net, ("trade", "path"), scatter_dimension=0, tiled=True)

    inverse = pl.pallas_call(
        inverse_kernel,
        out_shape=jax.ShapeDtypeStruct((dates, wide, wide), F32),
        in_specs=[vmem] * 3,
        out_specs=vmem,
        compiler_params=params,
        cost_estimate=pl.CostEstimate(flops=8 * 10**9, bytes_accessed=10**6, transcendentals=0),
        name="gram_inverse",
    )(all_start, all_shocks, all_weights)

    totals = lax.all_gather(share, "path", axis=0, tiled=True)

    exposure, expected = pl.pallas_call(
        exposure_kernel,
        out_shape=(
            jax.ShapeDtypeStruct((dates, owned, paths), F32),
            jax.ShapeDtypeStruct((dates, owned), F32),
        ),
        in_specs=[vmem] * 6,
        out_specs=(vmem, vmem),
        compiler_params=params,
        cost_estimate=pl.CostEstimate(flops=2 * 10**9, bytes_accessed=2 * 10**6, transcendentals=0),
        name="set_exposure",
    )(totals, inverse, all_start, all_shocks, all_weights, thresholds[:, None])
    return (exposure, expected)


def solution(mesh):
    placed = (
        P("path", None),
        P(None, "path", None),
        P(None, "trade"),
        P("trade"),
        P("trade"),
        P("trade"),
        P(),
        P("path"),
        P("trade"),
    )
    return jax.shard_map(
        body,
        mesh=mesh,
        in_specs=placed,
        out_specs=(P(None, "trade", "path"), P(None, "trade")),
        check_vma=False,
    )
```

profile of v0, /device:TPU:0, one launch (start us, length us, event | category | flops | bytes accessed | tf_op | source)
XLA Modules:
  0.0 191.5 jit_solution(4231276295046383541)
XLA Ops:
  7.2 0.0 reduce-scatter.2.cloned.1.call-start
  7.2 25.0 %net_moments.1 = f32[1024,128]{1,0:T(8,128)} custom-call(s32[4]{0:T(128)} %counts_ref.1, f32[32,512]{1,0:T(8,128)} %bitcast.14, f32[2,32,512]{2,1,0:T(8,128)} %bitcast.16, s32[1,512]{1,0:T(1,128)} %bitcast.18, f32[32,8192]{1,0:T(8,128)} %load_ref.1, f32[1,8192]{1,0:T(1,128)} %bitcast.21, f32[1,8192]{1,0:T(1,128)} %bitcast.22, s32[1,8192]{1,0:T(1,128)} %bitcast.23), custom_call_target="tpu_custom_call" | custom-call | flops 16000000000 | bytes 4000000 | tf_op jit(solution)/shard_map/net_moments/pallas_call | solution.py:212
  32.2 0.0 copy-start.1
  32.2 0.0 copy-start.2
  32.2 0.0 reduce-scatter.2.cloned.1.call-update
  32.3 0.9 copy-done.1
  33.1 0.0 copy-start.3
  33.1 0.7 copy-done.3
  33.8 0.0 copy-start
  33.8 0.8 copy.12.limits_ref
  34.6 0.0 copy-done.2
  34.6 11.3 %all-gather.2.weights_ref = s32[8,1,512]{2,1,0:T(1,128)} all-gather(s32[1,1,512]{2,1,0:T(1,128)S(1)} %bitcast.19), channel_id=3, replica_groups=mesh['trade'=4,'path'=8] {'path'}, dimensions={0}, use_global_device_ids=true | all-gather | bytes 18432 | tf_op jit(solution)/shard_map/all_gather | solution.py:210
  45.9 0.0 copy-done
  45.9 10.9 %all-gather = f32[256,512]{1,0:T(8,128)} all-gather(f32[32,512]{1,0:T(8,128)S(1)} %bitcast.15), channel_id=2, replica_groups=mesh['trade'=4,'path'=8] {'path'}, dimensions={0}, use_global_device_ids=true | all-gather | bytes 589824 | tf_op jit(solution)/shard_map/all_gather | solution.py:207
  56.8 10.0 %all_gather.18 = f32[8,32,512]{2,1,0:T(8,128)} all-gather(f32[1,32,512]{2,1,0:T(8,128)S(1)} %slice.4), channel_id=1, replica_groups=mesh['trade'=4,'path'=8] {'path'}, dimensions={0}, use_global_device_ids=true | all-gather | bytes 589824 | tf_op jit(solution)/shard_map/all_gather | solution.py:208
  66.8 10.6 %gram_inverse.1.inverse_ref = f32[2,64,64]{2,1,0:T(8,128)} custom-call(f32[8,32,512]{2,1,0:T(8,128)} %bitcast.10, f32[1,8,32,512]{3,2,1,0:T(8,128)} %bitcast.12, s32[8,1,512]{2,1,0:T(1,128)} %all-gather.2.weights_ref), custom_call_target="tpu_custom_call" | custom-call | flops 8000000000 | bytes 1000000 | tf_op jit(solution)/shard_map/gram_inverse/pallas_call | solution.py:231
  77.4 91.9 %reduce-scatter.2.cloned.1.call-done = f32[32,128]{1,0:T(8,128)} async-done(((f32[1024,128]{1,0:T(8,128)}), f32[32,128]{1,0:T(8,128)}) %reduce-scatter.2.cloned.1.call-update) | async-done | bytes 16400 | tf_op jit(solution)/shard_map/reduce_scatter | solution.py:229
  169.4 10.0 %all_gather.15.totals_ref = f32[256,128]{1,0:T(8,128)} all-gather(f32[32,128]{1,0:T(8,128)} %reduce-scatter.2.cloned.1.call-done), channel_id=1, replica_groups=mesh['trade'=4,'path'=8] {'path'}, dimensions={0}, use_global_device_ids=true | all-gather | bytes 147456 | tf_op jit(solution)/shard_map/all_gather | solution.py:241
  179.3 5.4 %set_exposure.1 = (f32[2,256,512]{2,1,0:T(8,128)}, f32[2,256]{1,0:T(2,128)}) custom-call(f32[256,128]{1,0:T(8,128)} %all_gather.15.totals_ref, f32[2,64,64]{2,1,0:T(8,128)} %gram_inverse.1.inverse_ref, f32[8,32,512]{2,1,0:T(8,128)} %bitcast.11, f32[1,8,32,512]{3,2,1,0:T(8,128)} %bitcast.13, s32[8,1,512]{2,1,0:T(1,128)} %all-gather.2.weights_ref, ...), custom_call_target="tpu_custom_call" | custom-call | flops 2000000000 | bytes 2000000 | tf_op jit(solution)/shard_map/set_exposure/pallas_call | solution.py:243
  (1 shorter events, 0.0 us)
Async XLA Ops:
  7.2 162.2 %reduce-scatter.2.cloned.1.call-start = ((), (), s32[]{:S(2)}) async-start(), calls=%async_computation.1 | async-start | bytes 540672 | tf_op jit(solution)/shard_map/reduce_scatter | solution.py:229
  32.2 0.9 copy-start.1
  32.2 2.4 %copy-start.2 = (s32[512]{0:T(512)S(1)}, s32[512]{0:T(512)}, u32[]{:S(2)}) copy-start(s32[512]{0:T(512)} %param.16) | copy-start | bytes 6148
  33.1 0.7 copy-start.3
  33.8 12.1 %copy-start = (f32[512,32]{0,1:T(8,128)S(1)}, f32[512,32]{0,1:T(8,128)}, u32[]{:S(2)}) copy-start(f32[512,32]{0,1:T(8,128)} %param.9) | copy-start | bytes 196612
Sparse Core Ops, SparseCore 0:
  32.4 136.9 reduce-scatter.1
where the time goes:
time: 192 us
  waiting for transfers between devices  92 us (48%)
  blocking collectives  42.2 us (22%)
  Pallas kernels  41 us (21%)
  between operations  14 us (7%)
  local copies, waits for them, and re-layouts  2.36 us (1%)
    reduce_scatter x1, waiting for transfers between devices, body(): lax.psum_scatter(net, ('trade', 'path'), scatter_dimension=0, tiled=True)  91.9 us
    pallas_call x1, Pallas kernels, body(): pl.pallas_call(moment_kernel, out_shape=jax.ShapeDtypeStruct((sets, dates...  25 us
    all_gather x1, blocking collectives, body(): all_weights = lax.all_gather(weights_row, 'path')  11.3 us
    all_gather x1, blocking collectives, body(): all_start = lax.all_gather(start_t, 'path')  10.9 us
    pallas_call x1, Pallas kernels, body(): pl.pallas_call(inverse_kernel, out_shape=jax.ShapeDtypeStruct((dates, wid...  10.6 us
    all_gather x1, blocking collectives, body(): lax.all_gather(shocks_t[date], 'path')  10 us
    all_gather x1, blocking collectives, body(): totals = lax.all_gather(share, 'path', axis=0, tiled=True)  9.96 us
    pallas_call x1, Pallas kernels, body(): pl.pallas_call(exposure_kernel, out_shape=(jax.ShapeDtypeStruct((dates, o...  5.39 us
  transfers between devices with their start and end apart: 1, of which 1 were waited for; matrix products, arithmetic and copies ran while one was open for 0% of the time, Pallas kernels for 6%

commit v1 on v0

--- a/solution.py
+++ b/solution.py
@@ -13,7 +13,7 @@
 BF16 = jnp.bfloat16
 TILE = 512
 DEPTH = 256
-VMEM_BYTES = 56 * 1024 * 1024
+MIB = 1024 * 1024
 NN = (((1,), (0,)), ((), ()))
 NT = (((1,), (1,)), ((), ()))
 
@@ -44,13 +44,16 @@
 
 def moment_kernel(
     counts_ref, start_ref, shocks_ref, weights_ref, load_ref, strike_ref, notional_ref, set_ref,
-    net_ref, states_scr, wide_scr, load_scr,
+    keep_ref, send_ref, states_scr, wide_scr, load_scr, net_ref,
+    *, groups, ranks,
 ):
     factors, paths = start_ref.shape
     dates = shocks_ref.shape[0]
     slots = load_ref.shape[1]
     sets = net_ref.shape[0]
-    filled = counts_ref[lax.axis_index("trade")]
+    group, rank = lax.axis_index("trade"), lax.axis_index("path")
+    filled = counts_ref[group]
+    rows_bits = log2(sets // (groups * ranks))
 
     weight_row = weights_ref[...].astype(F32)
     state = start_ref[...]
@@ -90,8 +93,13 @@
             his.append(hi)
             los.append(lo)
         stacked = jnp.concatenate(his + los, axis=0)
+        set_ids = set_ref[:, cols]
+        to_rank = ((set_ids >> rows_bits) & (ranks - 1)) ^ rank
+        to_group = (set_ids >> (rows_bits + log2(ranks))) ^ group
+        places = (to_rank & 1) * (ranks // 2) + (to_rank >> 1)
+        places = ((places * groups + to_group) << rows_bits) + (set_ids & ((1 << rows_bits) - 1))
         one_hot = jnp.where(
-            lax.broadcasted_iota(jnp.int32, (sets, TILE), 0) == set_ref[:, cols], 1.0, 0.0
+            lax.broadcasted_iota(jnp.int32, (sets, TILE), 0) == places, 1.0, 0.0
         ).astype(BF16)
         summed = mm(one_hot, stacked, NT)
         half = summed.shape[1] // 2
@@ -99,27 +107,44 @@
         return carry
 
     lax.fori_loop(0, slots // TILE, step, 0)
-
-
-def inverse_kernel(start_ref, shock_ref, weights_ref, inverse_ref):
-    blocks, factors, _ = start_ref.shape
-    dates = inverse_ref.shape[0]
+    keep_ref[...] = net_ref[: sets // 2]
+    send_ref[...] = net_ref[sets // 2 :]
+
+
+def add_kernel(count, *refs):
+    outs = refs[count:]
+    rows = outs[0].shape[0]
+    for part, out in enumerate(outs):
+        cut = pl.ds(part * rows, rows)
+        total = refs[0][cut, :]
+        for ref in refs[1:count]:
+            total = total + ref[cut, :]
+        out[...] = total
+
+
+def states_of(ref, factors, dates):
+    state = ref[:factors, :]
+    yield state
+    for date in range(1, dates):
+        state = 0.8 * state + 0.6 * ref[date * factors : (date + 1) * factors, :]
+        yield state
+
+
+def weights_of(ref, factors, dates):
+    return ref[dates * factors : dates * factors + 1, :]
+
+
+def inverse_kernel(factors, dates, *refs):
+    blocks, inverse_ref = refs[:-1], refs[-1]
     wide = 2 * factors
     sub = lax.broadcasted_iota(jnp.int32, (wide, wide), 0)
     lane = lax.broadcasted_iota(jnp.int32, (wide, wide), 1)
-
-    def step(block, grams):
-        weight_row = weights_ref[block].astype(F32)
-        state = start_ref[block]
-        results = []
-        for date in range(dates):
-            if date > 0:
-                state = 0.8 * state + 0.6 * shock_ref[date - 1, block]
+    grams = [jnp.zeros((wide, wide), F32) for _ in range(dates)]
+    for block in blocks:
+        weight_row = weights_of(block, factors, dates)
+        for date, state in enumerate(states_of(block, factors, dates)):
             basis = basis_rows(state)
-            results.append(grams[date] + mm_full(basis * weight_row, basis, NT))
-        return tuple(results)
-
-    grams = lax.fori_loop(0, blocks, step, tuple(jnp.zeros((wide, wide), F32) for _ in range(dates)))
+            grams[date] = grams[date] + mm_full(basis * weight_row, basis, NT)
     work = list(grams)
     for k in range(wide):
         for date in range(dates):
@@ -135,54 +160,58 @@
         inverse_ref[date] = approx + mm_full(approx, eye - mm_full(grams[date], approx))
 
 
-def exposure_kernel(
-    totals_ref, inverse_ref, start_ref, shock_ref, weights_ref, limits_ref, exposure_ref, expected_ref
-):
-    blocks, factors, paths = start_ref.shape
-    dates = inverse_ref.shape[0]
+def exposure_kernel(factors, dates, ranks, *refs):
+    shares, blocks = refs[:ranks], refs[ranks : 2 * ranks]
+    inverse_ref, limits_ref, exposure_ref, expected_ref, totals_scr = refs[2 * ranks :]
     wide = 2 * factors
-    mine = lax.axis_index("path")
+    paths = blocks[0].shape[1]
+    rank = lax.axis_index("path")
+    rows = shares[0].shape[0]
+    for away, share in enumerate(shares):
+        totals_scr[pl.ds(pl.multiple_of((rank ^ away) * rows, rows), rows), :] = share[...]
     limits = 0.25 * limits_ref[...].astype(F32)
     coeffs = []
     for date in range(dates):
-        hi, lo = split2(mm_full(totals_ref[:, date * wide : (date + 1) * wide], inverse_ref[date]))
+        hi, lo = split2(mm_full(totals_scr[:, date * wide : (date + 1) * wide], inverse_ref[date]))
         coeffs.append(jnp.concatenate([hi, hi, lo], axis=1))
-
-    def netted(block):
-        state = start_ref[block]
-        results = []
-        for date in range(dates):
-            if date > 0:
-                state = 0.8 * state + 0.6 * shock_ref[date - 1, block]
+    sums = [jnp.zeros((limits.shape[0], 128), F32) for _ in range(dates)]
+    total = jnp.zeros((1, 1), F32)
+    for away, block in enumerate(blocks):
+        weight_row = weights_of(block, factors, dates)
+        total = total + jnp.sum(weight_row, keepdims=True)
+        for date, state in enumerate(states_of(block, factors, dates)):
             hi, lo = split2(basis_rows(state))
             value = mm(coeffs[date], jnp.concatenate([hi, lo, hi], axis=0))
-            results.append(jnp.maximum(value - limits, 0.0))
-        return results
-
-    own = netted(mine)
-    for date in range(dates):
-        exposure_ref[date] = own[date]
-
-    def step(block, carry):
-        weight_row = weights_ref[block].astype(F32)
-        sums, total = carry
-        results = []
-        parts = netted(block)
-        for date in range(dates):
-            product = parts[date] * weight_row
-            partial = sums[date]
+            value = jnp.maximum(value - limits, 0.0)
+            if away == 0:
+                exposure_ref[date] = value
+            product = value * weight_row
             for c in range(paths // 128):
-                partial = partial + product[:, c * 128 : (c + 1) * 128]
-            results.append(partial)
-        return (tuple(results), total + jnp.sum(weight_row, keepdims=True))
-
-    sets = limits.shape[0]
-    sums, total = lax.fori_loop(
-        0, blocks, step,
-        (tuple(jnp.zeros((sets, 128), F32) for _ in range(dates)), jnp.zeros((1, 1), F32)),
-    )
+                sums[date] = sums[date] + product[:, c * 128 : (c + 1) * 128]
     for date in range(dates):
         expected_ref[date : date + 1, :] = jnp.sum(sums[date].T, axis=0, keepdims=True) / total
+
+
+def log2(n):
+    assert n & (n - 1) == 0
+    return n.bit_length() - 1
+
+
+def swap(x, axis, away):
+    return lax.ppermute(x, axis, [(i, i ^ away) for i in range(lax.axis_size(axis))])
+
+
+def added(arrays, parts):
+    rows, cols = arrays[0].shape
+    vmem = pl.BlockSpec(memory_space=pltpu.VMEM)
+    return pl.pallas_call(
+        functools.partial(add_kernel, len(arrays)),
+        out_shape=[jax.ShapeDtypeStruct((rows // parts, cols), F32)] * parts,
+        in_specs=[vmem] * len(arrays),
+        out_specs=[vmem] * parts,
+        compiler_params=pltpu.CompilerParams(vmem_limit_bytes=4 * MIB),
+        name="add_parts",
+    )(*arrays)
 
 
 def body(
@@ -202,56 +231,64 @@
     weights_row = weights[None, :]
     vmem = pl.BlockSpec(memory_space=pltpu.VMEM)
     smem = pl.BlockSpec(memory_space=pltpu.SMEM)
-    params = pltpu.CompilerParams(vmem_limit_bytes=VMEM_BYTES)
-
-    all_start = lax.all_gather(start_t, "path")
-    all_shocks = [lax.all_gather(shocks_t[date], "path") for date in range(dates - 1)]
-    all_shocks = jnp.stack(all_shocks) if len(all_shocks) > 1 else all_shocks[0][None]
-    all_weights = lax.all_gather(weights_row, "path")
-
-    net = pl.pallas_call(
-        moment_kernel,
-        out_shape=jax.ShapeDtypeStruct((sets, dates * wide), F32),
+
+    packed = jnp.concatenate(
+        [start_t]
+        + [shocks_t[date] for date in range(dates - 1)]
+        + [jnp.broadcast_to(weights_row.astype(F32), (8, paths))],
+        axis=0,
+    )
+    blocks = [packed] + [swap(packed, "path", away) for away in range(1, ranks)]
+
+    keep, send = pl.pallas_call(
+        functools.partial(moment_kernel, groups=groups, ranks=ranks),
+        out_shape=[jax.ShapeDtypeStruct((sets // 2, dates * wide), F32)] * 2,
         in_specs=[smem] + [vmem] * 7,
-        out_specs=vmem,
+        out_specs=[vmem] * 2,
         scratch_shapes=[
             pltpu.VMEM((dates * paths, DEPTH), BF16),
             pltpu.VMEM((dates, 2 * wide, paths), BF16),
             pltpu.VMEM((DEPTH, TILE), BF16),
+            pltpu.VMEM((sets, dates * wide), F32),
         ],
-        compiler_params=params,
+        compiler_params=pltpu.CompilerParams(vmem_limit_bytes=20 * MIB),
         cost_estimate=pl.CostEstimate(flops=16 * 10**9, bytes_accessed=4 * 10**6, transcendentals=0),
         name="net_moments",
     )(
         live_counts, start_t, shocks_t, weights_row, loadings, strikes[None, :], notionals[None, :],
         trade_set[None, :],
     )
-    share = lax.psum_scatter(net, ("trade", "path"), scatter_dimension=0, tiled=True)
+    got = swap(send, "path", 1)
+    chips = added([keep, got], ranks // 2)
+    got = [swap(chips[away], "path", 2 * away) for away in range(1, ranks // 2)]
+    by_group = added([chips[0]] + got, groups)
+    got = [swap(by_group[away], "trade", away) for away in range(1, groups)]
+    (share,) = added([by_group[0]] + got, 1)
+    shares = [share] + [swap(share, "path", away) for away in range(1, ranks)]
 
     inverse = pl.pallas_call(
-        inverse_kernel,
+        functools.partial(inverse_kernel, factors, dates),
         out_shape=jax.ShapeDtypeStruct((dates, wide, wide), F32),
-        in_specs=[vmem] * 3,
+        in_specs=[vmem] * ranks,
         out_specs=vmem,
-        compiler_params=params,
+        compiler_params=pltpu.CompilerParams(vmem_limit_bytes=8 * MIB),
         cost_estimate=pl.CostEstimate(flops=8 * 10**9, bytes_accessed=10**6, transcendentals=0),
         name="gram_inverse",
-    )(all_start, all_shocks, all_weights)
-
-    totals = lax.all_gather(share, "path", axis=0, tiled=True)
+    )(*blocks)
 
     exposure, expected = pl.pallas_call(
-        exposure_kernel,
+        functools.partial(exposure_kernel, factors, dates, ranks),
         out_shape=(
             jax.ShapeDtypeStruct((dates, owned, paths), F32),
             jax.ShapeDtypeStruct((dates, owned), F32),
         ),
-        in_specs=[vmem] * 6,
+        in_specs=[vmem] * (2 * ranks + 2),
         out_specs=(vmem, vmem),
-        compiler_params=params,
+        scratch_shapes=[pltpu.VMEM((owned, dates * wide), F32)],
+        compiler_params=pltpu.CompilerParams(vmem_limit_bytes=16 * MIB),
         cost_estimate=pl.CostEstimate(flops=2 * 10**9, bytes_accessed=2 * 10**6, transcendentals=0),
         name="set_exposure",
-    )(totals, inverse, all_start, all_shocks, all_weights, thresholds[:, None])
+    )(*shares, *blocks, inverse, thresholds[:, None])
     return (exposure, expected)
 
 

time: 192 us -> 74.9 us (0.39)
  waiting for transfers between devices: 92 us -> 10.5 us
  blocking collectives: 42.2 us -> 0 us
  starting transfers between devices: 0.04 us -> 22.9 us
  between operations: 14 us -> 0.78 us
  Pallas kernels: 41 us -> 34.2 us
  local copies, waits for them, and re-layouts: 2.36 us -> 6.06 us
    reduce_scatter x1 -> x0, waiting for transfers between devices: 91.9 us -> none  [body(): lax.psum_scatter(net, ('trade', 'path'), scatter_dimension=0, tiled=True)]
    all_gather x4 -> x0, blocking collectives: 42.2 us -> none  [the longest x1 11.3 us: body(): all_weights = lax.all_gather(weights_row, 'path')]
    ppermute x0 -> x21, starting transfers between devices: none -> 22.9 us  [swap(): lax.ppermute(x, axis, [(i, i ^ away) for i in range(lax.axis_size(axis))])]
    ppermute x0 -> x21, waiting for transfers between devices: none -> 10.5 us  [swap(): lax.ppermute(x, axis, [(i, i ^ away) for i in range(lax.axis_size(axis))])]
    pallas_call x3 -> x6, Pallas kernels: 41 us -> 34.2 us  [the longest x1 23.5 us: body(): pl.pallas_call(functools.partial(moment_kernel, groups=groups, ranks=rank...]
    unnamed x8 -> x18, local copies, waits for them, and re-layouts: 1.56 us -> 5.91 us
  transfers between devices with their start and end apart: 1 -> 21, of which waited for: 1 -> 5; matrix products, arithmetic and copies ran while one was open for 0% -> 0% of each run, Pallas kernels for 6% -> 10%
where the time goes in v1:
time: 74.9 us; the launch traced here: 74.4 us
  Pallas kernels  34.2 us (46%)
  starting transfers between devices  22.9 us (31%)
  waiting for transfers between devices  10.5 us (14%)
  local copies, waits for them, and re-layouts  6.06 us (8%)
  between operations  0.78 us (1%)
    pallas_call x1, Pallas kernels, body(): pl.pallas_call(functools.partial(moment_kernel, groups=groups, ranks=rank...  23.5 us
    ppermute x21, starting transfers between devices, swap(): lax.ppermute(x, axis, [(i, i ^ away) for i in range(lax.axis_size(axis))])  22.9 us
    ppermute x21, waiting for transfers between devices, swap(): lax.ppermute(x, axis, [(i, i ^ away) for i in range(lax.axis_size(axis))])  10.5 us
    pallas_call x1, Pallas kernels, body(): pl.pallas_call(functools.partial(inverse_kernel, factors, dates), out_sha...  7.71 us
    unnamed x18, local copies, waits for them, and re-layouts  5.91 us
    pallas_call x1, Pallas kernels, body(): pl.pallas_call(functools.partial(exposure_kernel, factors, dates, ranks),...  2.96 us
  transfers between devices with their start and end apart: 21, of which 5 were waited for; matrix products, arithmetic and copies ran while one was open for 0% of the time, Pallas kernels for 10%

profile of v1, /device:TPU:0, one launch (start us, length us, event | category | flops | bytes accessed | tf_op | source)
XLA Modules:
  0.0 74.4 jit_solution(14103434555113327446)
XLA Ops:
  0.7 0.7 copy-done.2
  1.3 0.8 %copy-done = f32[512,32]{0,1:T(8,128)S(1)} copy-done((f32[512,32]{0,1:T(8,128)S(1)}, f32[512,32]{0,1:T(8,128)}, u32[]{:S(2)}) %copy-start) | copy-done | bytes 65560
  2.2 0.9 %copy-done.1 = f32[2,512,32]{1,2,0:T(8,128)S(1)} copy-done((f32[2,512,32]{1,2,0:T(8,128)S(1)}, f32[2,512,32]{1,2,0:T(8,128)}, u32[]{:S(2)}) %copy-start.1) | copy-done | bytes 131096
  3.1 1.2 %copy-done.3 = f32[32,8192]{1,0:T(8,128)S(1)} copy-done((f32[32,8192]{1,0:T(8,128)S(1)}, f32[32,8192]{1,0:T(8,128)}, u32[]{:S(2)}) %copy-start.3) | copy-done | bytes 1048600
  4.3 0.8 %copy-done.4 = f32[8192]{0:T(1024)S(1)} copy-done((f32[8192]{0:T(1024)S(1)}, f32[8192]{0:T(1024)}, u32[]{:S(2)}) %copy-start.4) | copy-done | bytes 32792
  5.0 0.8 %copy-done.5 = f32[8192]{0:T(1024)S(1)} copy-done((f32[8192]{0:T(1024)S(1)}, f32[8192]{0:T(1024)}, u32[]{:S(2)}) %copy-start.5) | copy-done | bytes 32792
  5.8 0.8 %copy-done.6 = s32[8192]{0:T(1024)S(1)} copy-done((s32[8192]{0:T(1024)S(1)}, s32[8192]{0:T(1024)}, u32[]{:S(2)}) %copy-start.6) | copy-done | bytes 32792
  6.6 23.5 %net_moments.1 = (f32[512,128]{1,0:T(8,128)S(1)}, f32[512,128]{1,0:T(8,128)S(1)}) custom-call(s32[4]{0:T(128)S(1)} %copy-done.7, f32[32,512]{1,0:T(8,128)S(1)} %bitcast.9, f32[2,32,512]{2,1,0:T(8,128)S(1)} %bitcast.11, s32[1,512]{1,0:T(1,128)S(1)} %bitcast.13, f32[32,8192]{1,0:T(8,128)S(1)} %copy-done.3, f32[1,8192]{1,0:T(1,128)S(1)} %bitcast.14, ...), custom_call_target="tpu_custom_call" | custom-call | flops 16000000000 | bytes 4000000 | tf_op jit(solution)/shard_map/net_moments/pallas_call | solution.py:243
  30.0 0.5 collective-permute-start
  30.6 3.6 %collective-permute-start.20 = (f32[72,512]{1,0:T(8,128)S(1)}, f32[72,512]{1,0:T(8,128)S(1)}, u32[]{:S(2)}, u32[]{:S(2)}) collective-permute-start(f32[72,512]{1,0:T(8,128)S(1)} %pad_maximum_fusion.refs_0_.refs_8_), channel_id=1, source_target_pairs={{0,7},{1,6},{2,5},{3,4},{4,3},{5,2},{6,1},{7,0},{8,15},{9,14},{10,... | collective-permute-start | bytes 442376 | tf_op jit(solution)/shard_map/ppermute | solution.py:201
  34.2 0.0 collective-permute-start.19
  34.3 0.0 collective-permute-done.refs_1_
  34.3 2.0 %collective-permute-start.1 = (f32[128,128]{1,0:T(8,128)S(1)}, f32[128,128]{1,0:T(8,128)S(1)}, u32[]{:S(2)}, u32[]{:S(2)}) collective-permute-start(f32[128,128]{1,0:T(8,128)S(1)} %get-tuple-element.15), channel_id=1, source_target_pairs={{0,2},{1,3},{2,0},{3,1},{4,6},{5,7},{6,4},{7,5},{8,10},{9,11},{10,... | collective-permute-start | bytes 196616 | tf_op jit(solution)/shard_map/ppermute | solution.py:201
  36.3 1.5 %collective-permute-start.2 = (f32[128,128]{1,0:T(8,128)S(1)}, f32[128,128]{1,0:T(8,128)S(1)}, u32[]{:S(2)}, u32[]{:S(2)}) collective-permute-start(f32[128,128]{1,0:T(8,128)S(1)} %get-tuple-element.16), channel_id=1, source_target_pairs={{0,4},{1,5},{2,6},{3,7},{4,0},{5,1},{6,2},{7,3},{8,12},{9,13},{10,... | collective-permute-start | bytes 196616 | tf_op jit(solution)/shard_map/ppermute | solution.py:201
  37.8 0.0 collective-permute-start.3
  37.8 6.2 %collective-permute-done.1.refs_1_ = f32[128,128]{1,0:T(8,128)S(1)} collective-permute-done((f32[128,128]{1,0:T(8,128)S(1)}, f32[128,128]{1,0:T(8,128)S(1)}, u32[]{:S(2)}, u32[]{:S(2)}) %collective-permute-start.1) | collective-permute-done | bytes 65568 | tf_op jit(solution)/shard_map/ppermute | solution.py:201
  44.0 0.0 collective-permute-done.2.refs_2_
  44.0 0.6 collective-permute-done.3.refs_3_
  44.7 1.7 %collective-permute-start.4 = (f32[32,128]{1,0:T(8,128)S(1)}, f32[32,128]{1,0:T(8,128)S(1)}, u32[]{:S(2)}, u32[]{:S(2)}) collective-permute-start(f32[32,128]{1,0:T(8,128)S(1)} %get-tuple-element.19), channel_id=1, source_target_pairs={{0,8},{8,0},{16,24},{24,16},{1,9},{9,1},{17,25},{25,17},{2,10},{10... | collective-permute-start | bytes 49160 | tf_op jit(solution)/shard_map/ppermute | solution.py:201
  46.4 2.6 %collective-permute-start.5 = (f32[32,128]{1,0:T(8,128)S(1)}, f32[32,128]{1,0:T(8,128)S(1)}, u32[]{:S(2)}, u32[]{:S(2)}) collective-permute-start(f32[32,128]{1,0:T(8,128)S(1)} %get-tuple-element.20), channel_id=1, source_target_pairs={{0,16},{8,24},{16,0},{24,8},{1,17},{9,25},{17,1},{25,9},{2,18},{10... | collective-permute-start | bytes 49160 | tf_op jit(solution)/shard_map/ppermute | solution.py:201
  49.0 0.1 collective-permute-start.6
  49.1 0.0 collective-permute-done.20.refs_7_.refs_15_
  49.1 0.0 collective-permute-start.18
  49.1 0.0 collective-permute-done.19.refs_6_.refs_14_
  49.1 1.7 %collective-permute-start.17 = (f32[72,512]{1,0:T(8,128)S(1)}, f32[72,512]{1,0:T(8,128)S(1)}, u32[]{:S(2)}, u32[]{:S(2)}) collective-permute-start(f32[72,512]{1,0:T(8,128)S(1)} %pad_maximum_fusion.refs_0_.refs_8_), channel_id=1, source_target_pairs={{0,4},{1,5},{2,6},{3,7},{4,0},{5,1},{6,2},{7,3},{8,12},{9,13},{10,... | collective-permute-start | bytes 442376 | tf_op jit(solution)/shard_map/ppermute | solution.py:201
  50.8 0.0 collective-permute-done.4.refs_1_
  50.8 1.4 %collective-permute-start.16 = (f32[72,512]{1,0:T(8,128)S(1)}, f32[72,512]{1,0:T(8,128)S(1)}, u32[]{:S(2)}, u32[]{:S(2)}) collective-permute-start(f32[72,512]{1,0:T(8,128)S(1)} %pad_maximum_fusion.refs_0_.refs_8_), channel_id=1, source_target_pairs={{0,3},{1,2},{2,1},{3,0},{4,7},{5,6},{6,5},{7,4},{8,11},{9,10},{10,... | collective-permute-start | bytes 442376 | tf_op jit(solution)/shard_map/ppermute | solution.py:201
  52.2 0.0 collective-permute-done.5.refs_2_
  52.2 0.4 collective-permute-start.15
  52.6 1.9 %collective-permute-done.6.refs_3_ = f32[32,128]{1,0:T(8,128)S(1)} collective-permute-done((f32[32,128]{1,0:T(8,128)S(1)}, f32[32,128]{1,0:T(8,128)S(1)}, u32[]{:S(2)}, u32[]{:S(2)}) %collective-permute-start.6) | collective-permute-done | bytes 16416 | tf_op jit(solution)/shard_map/ppermute | solution.py:201
  54.5 0.0 collective-permute-start.14
  54.5 0.0 copy-start.8
  54.6 0.5 collective-permute-done.18.refs_5_.refs_13_
  55.1 2.1 %collective-permute-start.13 = (f32[32,128]{1,0:T(8,128)S(1)}, f32[32,128]{1,0:T(8,128)S(1)}, u32[]{:S(2)}, u32[]{:S(2)}) collective-permute-start(f32[32,128]{1,0:T(8,128)S(1)} %add_parts.5.refs_0_), channel_id=1, source_target_pairs={{0,7},{1,6},{2,5},{3,4},{4,3},{5,2},{6,1},{7,0},{8,15},{9,14},{10,... | collective-permute-start | bytes 49160 | tf_op jit(solution)/shard_map/ppermute | solution.py:201
  57.2 1.2 %collective-permute-done.17.refs_4_.refs_12_ = f32[72,512]{1,0:T(8,128)S(1)} collective-permute-done((f32[72,512]{1,0:T(8,128)S(1)}, f32[72,512]{1,0:T(8,128)S(1)}, u32[]{:S(2)}, u32[]{:S(2)}) %collective-permute-start.17) | collective-permute-done | bytes 147488 | tf_op jit(solution)/shard_map/ppermute | solution.py:201
  58.4 0.7 collective-permute-start.12
  59.1 0.1 copy.11.refs_17_
  59.3 0.0 collective-permute-done.16.refs_3_.refs_11_
  59.3 1.8 %collective-permute-start.11 = (f32[32,128]{1,0:T(8,128)S(1)}, f32[32,128]{1,0:T(8,128)S(1)}, u32[]{:S(2)}, u32[]{:S(2)}) collective-permute-start(f32[32,128]{1,0:T(8,128)S(1)} %add_parts.5.refs_0_), channel_id=1, source_target_pairs={{0,5},{1,4},{2,7},{3,6},{4,1},{5,0},{6,3},{7,2},{8,13},{9,12},{10,... | collective-permute-start | bytes 49160 | tf_op jit(solution)/shard_map/ppermute | solution.py:201
  61.1 0.7 collective-permute-start.10
  61.8 0.1 collective-permute-start.9
  61.9 1.6 %collective-permute-start.8 = (f32[32,128]{1,0:T(8,128)S(1)}, f32[32,128]{1,0:T(8,128)S(1)}, u32[]{:S(2)}, u32[]{:S(2)}) collective-permute-start(f32[32,128]{1,0:T(8,128)S(1)} %add_parts.5.refs_0_), channel_id=1, source_target_pairs={{0,2},{1,3},{2,0},{3,1},{4,6},{5,7},{6,4},{7,5},{8,10},{9,11},{10,... | collective-permute-start | bytes 49160 | tf_op jit(solution)/shard_map/ppermute | solution.py:201
  63.5 0.1 collective-permute-start.7
  63.7 7.7 %gram_inverse.1.refs_16_ = f32[2,64,64]{2,1,0:T(8,128)S(1)} custom-call(f32[72,512]{1,0:T(8,128)S(1)} %pad_maximum_fusion.refs_0_.refs_8_, f32[72,512]{1,0:T(8,128)S(1)} %collective-permute-done.14.refs_1_.refs_9_, f32[72,512]{1,0:T(8,128)S(1)} %collective-permute-done.15.refs_2_.refs_10_, f32[72,512]{1,0:T(8,128)S(1)} %collective-permute-done.16.refs_3_.refs_11_, ...), custom_call_target="tpu_custom_call" | custom-call | flops 8000000000 | bytes 1000000 | tf_op jit(solution)/shard_map/gram_inverse/pallas_call | solution.py:269
  71.4 0.0 collective-permute-done.11.refs_5_
  71.4 0.0 collective-permute-done.8.refs_2_
  71.4 0.0 collective-permute-done.7.refs_1_
  71.5 3.0 %set_exposure.1 = (f32[2,256,512]{2,1,0:T(8,128)}, f32[2,256]{1,0:T(2,128)}) custom-call(f32[32,128]{1,0:T(8,128)S(1)} %add_parts.5.refs_0_, f32[32,128]{1,0:T(8,128)S(1)} %collective-permute-done.7.refs_1_, f32[32,128]{1,0:T(8,128)S(1)} %collective-permute-done.8.refs_2_, f32[32,128]{1,0:T(8,128)S(1)} %collective-permute-done.9.refs_3_, ...), custom_call_target="tpu_custom_call" | custom-call | flops 2000000000 | bytes 2000000 | tf_op jit(solution)/shard_map/set_exposure/pallas_call | solution.py:279
  (23 shorter events, 0.1 us)
Async XLA Ops:
  0.6 0.7 copy-start.2
  0.6 0.7 copy-start.7
  1.3 0.8 %copy-start = (f32[512,32]{0,1:T(8,128)S(1)}, f32[512,32]{0,1:T(8,128)}, u32[]{:S(2)}) copy-start(f32[512,32]{0,1:T(8,128)} %param.9) | copy-start | bytes 196612
  2.2 0.9 %copy-start.1 = (f32[2,512,32]{1,2,0:T(8,128)S(1)}, f32[2,512,32]{1,2,0:T(8,128)}, u32[]{:S(2)}) copy-start(f32[2,512,32]{1,2,0:T(8,128)} %param.10) | copy-start | bytes 393220
  3.1 1.2 %copy-start.3 = (f32[32,8192]{1,0:T(8,128)S(1)}, f32[32,8192]{1,0:T(8,128)}, u32[]{:S(2)}) copy-start(f32[32,8192]{1,0:T(8,128)} %load_ref.1) | copy-start | bytes 3145732
  4.3 0.8 %copy-start.4 = (f32[8192]{0:T(1024)S(1)}, f32[8192]{0:T(1024)}, u32[]{:S(2)}) copy-start(f32[8192]{0:T(1024)} %param.12) | copy-start | bytes 98308
  5.0 0.8 %copy-start.5 = (f32[8192]{0:T(1024)S(1)}, f32[8192]{0:T(1024)}, u32[]{:S(2)}) copy-start(f32[8192]{0:T(1024)} %param.13) | copy-start | bytes 98308
  5.8 0.8 %copy-start.6 = (s32[8192]{0:T(1024)S(1)}, s32[8192]{0:T(1024)}, u32[]{:S(2)}) copy-start(s32[8192]{0:T(1024)} %param.14) | copy-start | bytes 98308
  30.0 4.2 %collective-permute-start = (f32[512,128]{1,0:T(8,128)S(1)}, f32[512,128]{1,0:T(8,128)S(1)}, u32[]{:S(2)}, u32[]{:S(2)}) collective-permute-start(f32[512,128]{1,0:T(8,128)S(1)} %get-tuple-element.13), channel_id=1, source_target_pairs={{0,1},{1,0},{2,3},{3,2},{4,5},{5,4},{6,7},{7,6},{8,9},{9,8},{10,11... | collective-permute-start | bytes 786440 | tf_op jit(solution)/shard_map/ppermute | solution.py:201
  30.6 18.5 %collective-permute-start.20 = (f32[72,512]{1,0:T(8,128)S(1)}, f32[72,512]{1,0:T(8,128)S(1)}, u32[]{:S(2)}, u32[]{:S(2)}) collective-permute-start(f32[72,512]{1,0:T(8,128)S(1)} %pad_maximum_fusion.refs_0_.refs_8_), channel_id=1, source_target_pairs={{0,7},{1,6},{2,5},{3,4},{4,3},{5,2},{6,1},{7,0},{8,15},{9,14},{10,... | collective-permute-start | bytes 442376 | tf_op jit(solution)/shard_map/ppermute | solution.py:201
  34.2 14.9 %collective-permute-start.19 = (f32[72,512]{1,0:T(8,128)S(1)}, f32[72,512]{1,0:T(8,128)S(1)}, u32[]{:S(2)}, u32[]{:S(2)}) collective-permute-start(f32[72,512]{1,0:T(8,128)S(1)} %pad_maximum_fusion.refs_0_.refs_8_), channel_id=1, source_target_pairs={{0,6},{1,7},{2,4},{3,5},{4,2},{5,3},{6,0},{7,1},{8,14},{9,15},{10,... | collective-permute-start | bytes 442376 | tf_op jit(solution)/shard_map/ppermute | solution.py:201
  34.3 9.7 %collective-permute-start.1 = (f32[128,128]{1,0:T(8,128)S(1)}, f32[128,128]{1,0:T(8,128)S(1)}, u32[]{:S(2)}, u32[]{:S(2)}) collective-permute-start(f32[128,128]{1,0:T(8,128)S(1)} %get-tuple-element.15), channel_id=1, source_target_pairs={{0,2},{1,3},{2,0},{3,1},{4,6},{5,7},{6,4},{7,5},{8,10},{9,11},{10,... | collective-permute-start | bytes 196616 | tf_op jit(solution)/shard_map/ppermute | solution.py:201
  36.3 7.7 %collective-permute-start.2 = (f32[128,128]{1,0:T(8,128)S(1)}, f32[128,128]{1,0:T(8,128)S(1)}, u32[]{:S(2)}, u32[]{:S(2)}) collective-permute-start(f32[128,128]{1,0:T(8,128)S(1)} %get-tuple-element.16), channel_id=1, source_target_pairs={{0,4},{1,5},{2,6},{3,7},{4,0},{5,1},{6,2},{7,3},{8,12},{9,13},{10,... | collective-permute-start | bytes 196616 | tf_op jit(solution)/shard_map/ppermute | solution.py:201
  37.8 6.8 %collective-permute-start.3 = (f32[128,128]{1,0:T(8,128)S(1)}, f32[128,128]{1,0:T(8,128)S(1)}, u32[]{:S(2)}, u32[]{:S(2)}) collective-permute-start(f32[128,128]{1,0:T(8,128)S(1)} %get-tuple-element.17), channel_id=1, source_target_pairs={{0,6},{1,7},{2,4},{3,5},{4,2},{5,3},{6,0},{7,1},{8,14},{9,15},{10,... | collective-permute-start | bytes 196616 | tf_op jit(solution)/shard_map/ppermute | solution.py:201
  44.7 6.2 %collective-permute-start.4 = (f32[32,128]{1,0:T(8,128)S(1)}, f32[32,128]{1,0:T(8,128)S(1)}, u32[]{:S(2)}, u32[]{:S(2)}) collective-permute-start(f32[32,128]{1,0:T(8,128)S(1)} %get-tuple-element.19), channel_id=1, source_target_pairs={{0,8},{8,0},{16,24},{24,16},{1,9},{9,1},{17,25},{25,17},{2,10},{10... | collective-permute-start | bytes 49160 | tf_op jit(solution)/shard_map/ppermute | solution.py:201
  46.4 5.8 %collective-permute-start.5 = (f32[32,128]{1,0:T(8,128)S(1)}, f32[32,128]{1,0:T(8,128)S(1)}, u32[]{:S(2)}, u32[]{:S(2)}) collective-permute-start(f32[32,128]{1,0:T(8,128)S(1)} %get-tuple-element.20), channel_id=1, source_target_pairs={{0,16},{8,24},{16,0},{24,8},{1,17},{9,25},{17,1},{25,9},{2,18},{10... | collective-permute-start | bytes 49160 | tf_op jit(solution)/shard_map/ppermute | solution.py:201
  49.0 5.5 %collective-permute-start.6 = (f32[32,128]{1,0:T(8,128)S(1)}, f32[32,128]{1,0:T(8,128)S(1)}, u32[]{:S(2)}, u32[]{:S(2)}) collective-permute-start(f32[32,128]{1,0:T(8,128)S(1)} %get-tuple-element.21), channel_id=1, source_target_pairs={{0,24},{8,16},{16,8},{24,0},{1,25},{9,17},{17,9},{25,1},{2,26},{10... | collective-permute-start | bytes 49160 | tf_op jit(solution)/shard_map/ppermute | solution.py:201
  49.1 6.0 %collective-permute-start.18 = (f32[72,512]{1,0:T(8,128)S(1)}, f32[72,512]{1,0:T(8,128)S(1)}, u32[]{:S(2)}, u32[]{:S(2)}) collective-permute-start(f32[72,512]{1,0:T(8,128)S(1)} %pad_maximum_fusion.refs_0_.refs_8_), channel_id=1, source_target_pairs={{0,5},{1,4},{2,7},{3,6},{4,1},{5,0},{6,3},{7,2},{8,13},{9,12},{10,... | collective-permute-start | bytes 442376 | tf_op jit(solution)/shard_map/ppermute | solution.py:201
  49.1 9.3 %collective-permute-start.17 = (f32[72,512]{1,0:T(8,128)S(1)}, f32[72,512]{1,0:T(8,128)S(1)}, u32[]{:S(2)}, u32[]{:S(2)}) collective-permute-start(f32[72,512]{1,0:T(8,128)S(1)} %pad_maximum_fusion.refs_0_.refs_8_), channel_id=1, source_target_pairs={{0,4},{1,5},{2,6},{3,7},{4,0},{5,1},{6,2},{7,3},{8,12},{9,13},{10,... | collective-permute-start | bytes 442376 | tf_op jit(solution)/shard_map/ppermute | solution.py:201
  50.8 8.4 %collective-permute-start.16 = (f32[72,512]{1,0:T(8,128)S(1)}, f32[72,512]{1,0:T(8,128)S(1)}, u32[]{:S(2)}, u32[]{:S(2)}) collective-permute-start(f32[72,512]{1,0:T(8,128)S(1)} %pad_maximum_fusion.refs_0_.refs_8_), channel_id=1, source_target_pairs={{0,3},{1,2},{2,1},{3,0},{4,7},{5,6},{6,5},{7,4},{8,11},{9,10},{10,... | collective-permute-start | bytes 442376 | tf_op jit(solution)/shard_map/ppermute | solution.py:201
  52.2 8.9 %collective-permute-start.15 = (f32[72,512]{1,0:T(8,128)S(1)}, f32[72,512]{1,0:T(8,128)S(1)}, u32[]{:S(2)}, u32[]{:S(2)}) collective-permute-start(f32[72,512]{1,0:T(8,128)S(1)} %pad_maximum_fusion.refs_0_.refs_8_), channel_id=1, source_target_pairs={{0,2},{1,3},{2,0},{3,1},{4,6},{5,7},{6,4},{7,5},{8,10},{9,11},{10,... | collective-permute-start | bytes 442376 | tf_op jit(solution)/shard_map/ppermute | solution.py:201
  54.5 7.3 %collective-permute-start.14 = (f32[72,512]{1,0:T(8,128)S(1)}, f32[72,512]{1,0:T(8,128)S(1)}, u32[]{:S(2)}, u32[]{:S(2)}) collective-permute-start(f32[72,512]{1,0:T(8,128)S(1)} %pad_maximum_fusion.refs_0_.refs_8_), channel_id=1, source_target_pairs={{0,1},{1,0},{2,3},{3,2},{4,5},{5,4},{6,7},{7,6},{8,9},{9,8},{10,11... | collective-permute-start | bytes 442376 | tf_op jit(solution)/shard_map/ppermute | solution.py:201
  54.5 4.6 %copy-start.8 = (s32[256]{0:T(256)S(1)}, s32[256]{0:T(256)}, u32[]{:S(2)}) copy-start(s32[256]{0:T(256)} %param.17) | copy-start | bytes 3076
  55.1 6.8 %collective-permute-start.13 = (f32[32,128]{1,0:T(8,128)S(1)}, f32[32,128]{1,0:T(8,128)S(1)}, u32[]{:S(2)}, u32[]{:S(2)}) collective-permute-start(f32[32,128]{1,0:T(8,128)S(1)} %add_parts.5.refs_0_), channel_id=1, source_target_pairs={{0,7},{1,6},{2,5},{3,4},{4,3},{5,2},{6,1},{7,0},{8,15},{9,14},{10,... | collective-permute-start | bytes 49160 | tf_op jit(solution)/shard_map/ppermute | solution.py:201
  58.4 5.1 %collective-permute-start.12 = (f32[32,128]{1,0:T(8,128)S(1)}, f32[32,128]{1,0:T(8,128)S(1)}, u32[]{:S(2)}, u32[]{:S(2)}) collective-permute-start(f32[32,128]{1,0:T(8,128)S(1)} %add_parts.5.refs_0_), channel_id=1, source_target_pairs={{0,6},{1,7},{2,4},{3,5},{4,2},{5,3},{6,0},{7,1},{8,14},{9,15},{10,... | collective-permute-start | bytes 49160 | tf_op jit(solution)/shard_map/ppermute | solution.py:201
  59.3 12.1 %collective-permute-start.11 = (f32[32,128]{1,0:T(8,128)S(1)}, f32[32,128]{1,0:T(8,128)S(1)}, u32[]{:S(2)}, u32[]{:S(2)}) collective-permute-start(f32[32,128]{1,0:T(8,128)S(1)} %add_parts.5.refs_0_), channel_id=1, source_target_pairs={{0,5},{1,4},{2,7},{3,6},{4,1},{5,0},{6,3},{7,2},{8,13},{9,12},{10,... | collective-permute-start | bytes 49160 | tf_op jit(solution)/shard_map/ppermute | solution.py:201
  61.1 10.3 %collective-permute-start.10 = (f32[32,128]{1,0:T(8,128)S(1)}, f32[32,128]{1,0:T(8,128)S(1)}, u32[]{:S(2)}, u32[]{:S(2)}) collective-permute-start(f32[32,128]{1,0:T(8,128)S(1)} %add_parts.5.refs_0_), channel_id=1, source_target_pairs={{0,4},{1,5},{2,6},{3,7},{4,0},{5,1},{6,2},{7,3},{8,12},{9,13},{10,... | collective-permute-start | bytes 49160 | tf_op jit(solution)/shard_map/ppermute | solution.py:201
  61.8 9.6 %collective-permute-start.9 = (f32[32,128]{1,0:T(8,128)S(1)}, f32[32,128]{1,0:T(8,128)S(1)}, u32[]{:S(2)}, u32[]{:S(2)}) collective-permute-start(f32[32,128]{1,0:T(8,128)S(1)} %add_parts.5.refs_0_), channel_id=1, source_target_pairs={{0,3},{1,2},{2,1},{3,0},{4,7},{5,6},{6,5},{7,4},{8,11},{9,10},{10,... | collective-permute-start | bytes 49160 | tf_op jit(solution)/shard_map/ppermute | solution.py:201
  61.9 9.5 %collective-permute-start.8 = (f32[32,128]{1,0:T(8,128)S(1)}, f32[32,128]{1,0:T(8,128)S(1)}, u32[]{:S(2)}, u32[]{:S(2)}) collective-permute-start(f32[32,128]{1,0:T(8,128)S(1)} %add_parts.5.refs_0_), channel_id=1, source_target_pairs={{0,2},{1,3},{2,0},{3,1},{4,6},{5,7},{6,4},{7,5},{8,10},{9,11},{10,... | collective-permute-start | bytes 49160 | tf_op jit(solution)/shard_map/ppermute | solution.py:201
  63.5 7.9 %collective-permute-start.7 = (f32[32,128]{1,0:T(8,128)S(1)}, f32[32,128]{1,0:T(8,128)S(1)}, u32[]{:S(2)}, u32[]{:S(2)}) collective-permute-start(f32[32,128]{1,0:T(8,128)S(1)} %add_parts.5.refs_0_), channel_id=1, source_target_pairs={{0,1},{1,0},{2,3},{3,2},{4,5},{5,4},{6,7},{7,6},{8,9},{9,8},{10,11... | collective-permute-start | bytes 49160 | tf_op jit(solution)/shard_map/ppermute | solution.py:201

commit v2 on v1

--- a/solution.py
+++ b/solution.py
@@ -44,15 +44,14 @@
 
 def moment_kernel(
     counts_ref, start_ref, shocks_ref, weights_ref, load_ref, strike_ref, notional_ref, set_ref,
-    keep_ref, send_ref, states_scr, wide_scr, load_scr, net_ref,
+    net_ref, states_scr, wide_scr, load_scr,
     *, groups, ranks,
 ):
     factors, paths = start_ref.shape
     dates = shocks_ref.shape[0]
     slots = load_ref.shape[1]
     sets = net_ref.shape[0]
-    group, rank = lax.axis_index("trade"), lax.axis_index("path")
-    filled = counts_ref[group]
+    filled = counts_ref[lax.axis_index("trade")]
     rows_bits = log2(sets // (groups * ranks))
 
     weight_row = weights_ref[...].astype(F32)
@@ -94,10 +93,9 @@
             los.append(lo)
         stacked = jnp.concatenate(his + los, axis=0)
         set_ids = set_ref[:, cols]
-        to_rank = ((set_ids >> rows_bits) & (ranks - 1)) ^ rank
-        to_group = (set_ids >> (rows_bits + log2(ranks))) ^ group
-        places = (to_rank & 1) * (ranks // 2) + (to_rank >> 1)
-        places = ((places * groups + to_group) << rows_bits) + (set_ids & ((1 << rows_bits) - 1))
+        to_rank = (set_ids >> rows_bits) & (ranks - 1)
+        to_group = set_ids >> (rows_bits + log2(ranks))
+        places = ((to_rank * groups + to_group) << rows_bits) + (set_ids & ((1 << rows_bits) - 1))
         one_hot = jnp.where(
             lax.broadcasted_iota(jnp.int32, (sets, TILE), 0) == places, 1.0, 0.0
         ).astype(BF16)
@@ -107,19 +105,13 @@
         return carry
 
     lax.fori_loop(0, slots // TILE, step, 0)
-    keep_ref[...] = net_ref[: sets // 2]
-    send_ref[...] = net_ref[sets // 2 :]
-
-
-def add_kernel(count, *refs):
-    outs = refs[count:]
-    rows = outs[0].shape[0]
-    for part, out in enumerate(outs):
-        cut = pl.ds(part * rows, rows)
-        total = refs[0][cut, :]
-        for ref in refs[1:count]:
-            total = total + ref[cut, :]
-        out[...] = total
+
+
+def add_kernel(parts_ref, total_ref):
+    total = parts_ref[0]
+    for part in range(1, parts_ref.shape[0]):
+        total = total + parts_ref[part]
+    total_ref[...] = total
 
 
 def states_of(ref, factors, dates):
@@ -134,15 +126,14 @@
     return ref[dates * factors : dates * factors + 1, :]
 
 
-def inverse_kernel(factors, dates, *refs):
-    blocks, inverse_ref = refs[:-1], refs[-1]
+def inverse_kernel(factors, dates, blocks_ref, inverse_ref):
     wide = 2 * factors
     sub = lax.broadcasted_iota(jnp.int32, (wide, wide), 0)
     lane = lax.broadcasted_iota(jnp.int32, (wide, wide), 1)
     grams = [jnp.zeros((wide, wide), F32) for _ in range(dates)]
-    for block in blocks:
-        weight_row = weights_of(block, factors, dates)
-        for date, state in enumerate(states_of(block, factors, dates)):
+    for block in range(blocks_ref.shape[0]):
+        weight_row = weights_of(blocks_ref.at[block], factors, dates)
+        for date, state in enumerate(states_of(blocks_ref.at[block], factors, dates)):
             basis = basis_rows(state)
             grams[date] = grams[date] + mm_full(basis * weight_row, basis, NT)
     work = list(grams)
@@ -160,31 +151,31 @@
         inverse_ref[date] = approx + mm_full(approx, eye - mm_full(grams[date], approx))
 
 
-def exposure_kernel(factors, dates, ranks, *refs):
-    shares, blocks = refs[:ranks], refs[ranks : 2 * ranks]
-    inverse_ref, limits_ref, exposure_ref, expected_ref, totals_scr = refs[2 * ranks :]
+def exposure_kernel(
+    factors, dates, totals_ref, own_ref, blocks_ref, inverse_ref, limits_ref, exposure_ref, expected_ref
+):
     wide = 2 * factors
-    paths = blocks[0].shape[1]
-    rank = lax.axis_index("path")
-    rows = shares[0].shape[0]
-    for away, share in enumerate(shares):
-        totals_scr[pl.ds(pl.multiple_of((rank ^ away) * rows, rows), rows), :] = share[...]
+    paths = own_ref.shape[1]
     limits = 0.25 * limits_ref[...].astype(F32)
     coeffs = []
     for date in range(dates):
-        hi, lo = split2(mm_full(totals_scr[:, date * wide : (date + 1) * wide], inverse_ref[date]))
+        hi, lo = split2(mm_full(totals_ref[:, date * wide : (date + 1) * wide], inverse_ref[date]))
         coeffs.append(jnp.concatenate([hi, hi, lo], axis=1))
+
+    def exposures(block_ref):
+        for date, state in enumerate(states_of(block_ref, factors, dates)):
+            hi, lo = split2(basis_rows(state))
+            value = mm(coeffs[date], jnp.concatenate([hi, lo, hi], axis=0))
+            yield jnp.maximum(value - limits, 0.0)
+
+    for date, value in enumerate(exposures(own_ref)):
+        exposure_ref[date] = value
     sums = [jnp.zeros((limits.shape[0], 128), F32) for _ in range(dates)]
     total = jnp.zeros((1, 1), F32)
-    for away, block in enumerate(blocks):
-        weight_row = weights_of(block, factors, dates)
+    for block in range(blocks_ref.shape[0]):
+        weight_row = weights_of(blocks_ref.at[block], factors, dates)
         total = total + jnp.sum(weight_row, keepdims=True)
-        for date, state in enumerate(states_of(block, factors, dates)):
-            hi, lo = split2(basis_rows(state))
-            value = mm(coeffs[date], jnp.concatenate([hi, lo, hi], axis=0))
-            value = jnp.maximum(value - limits, 0.0)
-            if away == 0:
-                exposure_ref[date] = value
+        for date, value in enumerate(exposures(blocks_ref.at[block])):
             product = value * weight_row
             for c in range(paths // 128):
                 sums[date] = sums[date] + product[:, c * 128 : (c + 1) * 128]
@@ -197,21 +188,21 @@
     return n.bit_length() - 1
 
 
-def swap(x, axis, away):
-    return lax.ppermute(x, axis, [(i, i ^ away) for i in range(lax.axis_size(axis))])
-
-
-def added(arrays, parts):
-    rows, cols = arrays[0].shape
+def scatter_sum(parts, axis):
+    parts = lax.all_to_all(parts, axis, 0, 0)
     vmem = pl.BlockSpec(memory_space=pltpu.VMEM)
     return pl.pallas_call(
-        functools.partial(add_kernel, len(arrays)),
-        out_shape=[jax.ShapeDtypeStruct((rows // parts, cols), F32)] * parts,
-        in_specs=[vmem] * len(arrays),
-        out_specs=[vmem] * parts,
+        add_kernel,
+        out_shape=jax.ShapeDtypeStruct(parts.shape[1:], F32),
+        in_specs=[vmem],
+        out_specs=vmem,
         compiler_params=pltpu.CompilerParams(vmem_limit_bytes=4 * MIB),
         name="add_parts",
-    )(*arrays)
+    )(parts)
+
+
+def gather(x, axis):
+    return lax.all_to_all(jnp.broadcast_to(x, (lax.axis_size(axis), *x.shape)), axis, 0, 0)
 
 
 def body(
@@ -238,57 +229,51 @@
         + [jnp.broadcast_to(weights_row.astype(F32), (8, paths))],
         axis=0,
     )
-    blocks = [packed] + [swap(packed, "path", away) for away in range(1, ranks)]
-
-    keep, send = pl.pallas_call(
+    blocks = gather(packed, "path")
+
+    net = pl.pallas_call(
         functools.partial(moment_kernel, groups=groups, ranks=ranks),
-        out_shape=[jax.ShapeDtypeStruct((sets // 2, dates * wide), F32)] * 2,
+        out_shape=jax.ShapeDtypeStruct((sets, dates * wide), F32),
         in_specs=[smem] + [vmem] * 7,
-        out_specs=[vmem] * 2,
+        out_specs=vmem,
         scratch_shapes=[
             pltpu.VMEM((dates * paths, DEPTH), BF16),
             pltpu.VMEM((dates, 2 * wide, paths), BF16),
             pltpu.VMEM((DEPTH, TILE), BF16),
-            pltpu.VMEM((sets, dates * wide), F32),
         ],
-        compiler_params=pltpu.CompilerParams(vmem_limit_bytes=20 * MIB),
+        compiler_params=pltpu.CompilerParams(vmem_limit_bytes=58 * MIB),
         cost_estimate=pl.CostEstimate(flops=16 * 10**9, bytes_accessed=4 * 10**6, transcendentals=0),
         name="net_moments",
     )(
         live_counts, start_t, shocks_t, weights_row, loadings, strikes[None, :], notionals[None, :],
         trade_set[None, :],
     )
-    got = swap(send, "path", 1)
-    chips = added([keep, got], ranks // 2)
-    got = [swap(chips[away], "path", 2 * away) for away in range(1, ranks // 2)]
-    by_group = added([chips[0]] + got, groups)
-    got = [swap(by_group[away], "trade", away) for away in range(1, groups)]
-    (share,) = added([by_group[0]] + got, 1)
-    shares = [share] + [swap(share, "path", away) for away in range(1, ranks)]
+    by_group = scatter_sum(net.reshape(ranks, sets // ranks, dates * wide), "path")
+    share = scatter_sum(by_group.reshape(groups, owned // ranks, dates * wide), "trade")
+    totals = gather(share, "path").reshape(owned, dates * wide)
 
     inverse = pl.pallas_call(
         functools.partial(inverse_kernel, factors, dates),
         out_shape=jax.ShapeDtypeStruct((dates, wide, wide), F32),
-        in_specs=[vmem] * ranks,
+        in_specs=[vmem],
         out_specs=vmem,
         compiler_params=pltpu.CompilerParams(vmem_limit_bytes=8 * MIB),
         cost_estimate=pl.CostEstimate(flops=8 * 10**9, bytes_accessed=10**6, transcendentals=0),
         name="gram_inverse",
-    )(*blocks)
+    )(blocks)
 
     exposure, expected = pl.pallas_call(
-        functools.partial(exposure_kernel, factors, dates, ranks),
+        functools.partial(exposure_kernel, factors, dates),
         out_shape=(
             jax.ShapeDtypeStruct((dates, owned, paths), F32),
             jax.ShapeDtypeStruct((dates, owned), F32),
         ),
-        in_specs=[vmem] * (2 * ranks + 2),
+        in_specs=[vmem] * 5,
         out_specs=(vmem, vmem),
-        scratch_shapes=[pltpu.VMEM((owned, dates * wide), F32)],
         compiler_params=pltpu.CompilerParams(vmem_limit_bytes=16 * MIB),
         cost_estimate=pl.CostEstimate(flops=2 * 10**9, bytes_accessed=2 * 10**6, transcendentals=0),
         name="set_exposure",
-    )(*shares, *blocks, inverse, thresholds[:, None])
+    )(totals, packed, blocks, inverse, thresholds[:, None])
     return (exposure, expected)
 
 

time: 74.9 us -> 88.9 us (1.19)
  waiting for transfers between devices: 10.5 us -> 32 us
  starting transfers between devices: 22.9 us -> 17.2 us
  local copies, waits for them, and re-layouts: 6.06 us -> 1.98 us
  Pallas kernels: 34.2 us -> 36.4 us
    all_to_all x0 -> x4, waiting for transfers between devices: none -> 32 us  [the longest x2 16.6 us: gather(): lax.all_to_all(jnp.broadcast_to(x, (lax.axis_size(axis), *x.shape)), axis...]
    ppermute x21 -> x0, starting transfers between devices: 22.9 us -> none  [swap(): lax.ppermute(x, axis, [(i, i ^ away) for i in range(lax.axis_size(axis))])]
    all_to_all x0 -> x4, starting transfers between devices: none -> 17.2 us  [the longest x2 10.2 us: scatter_sum(): parts = lax.all_to_all(parts, axis, 0, 0)]
    ppermute x21 -> x0, waiting for transfers between devices: 10.5 us -> none  [swap(): lax.ppermute(x, axis, [(i, i ^ away) for i in range(lax.axis_size(axis))])]
    unnamed x18 -> x8, local copies, waits for them, and re-layouts: 5.91 us -> 0.02 us
    broadcast_in_dim x0 -> x2, local copies, waits for them, and re-layouts: none -> 1.83 us  [gather(): jnp.broadcast_to(x, (lax.axis_size(axis), *x.shape))]
    pallas_call x1, Pallas kernels: 23.5 us -> 25 us  [body(): pl.pallas_call(functools.partial(moment_kernel, groups=groups, ranks=rank...]
    pallas_call x4 -> x3, Pallas kernels: 3.01 us -> 3.61 us  [the longest x1 2.94 us: body(): pl.pallas_call(functools.partial(exposure_kernel, factors, dates), out_sh...]
  transfers between devices with their start and end apart: 21 -> 4, of which waited for: 5 -> 3; matrix products, arithmetic and copies ran while one was open for 0% -> 0% of each run, Pallas kernels for 10% -> 9%
where the time goes in v2:
time: 88.9 us; the launch traced here: 88.3 us
  Pallas kernels  36.4 us (41%)
  waiting for transfers between devices  32 us (36%)
  starting transfers between devices  17.2 us (19%)
  local copies, waits for them, and re-layouts  1.98 us (2%)
    pallas_call x1, Pallas kernels, body(): pl.pallas_call(functools.partial(moment_kernel, groups=groups, ranks=rank...  25 us
    all_to_all x2, waiting for transfers between devices, gather(): lax.all_to_all(jnp.broadcast_to(x, (lax.axis_size(axis), *x.shape)), axis...  16.6 us
    all_to_all x2, waiting for transfers between devices, scatter_sum(): parts = lax.all_to_all(parts, axis, 0, 0)  15.4 us
    all_to_all x2, starting transfers between devices, scatter_sum(): parts = lax.all_to_all(parts, axis, 0, 0)  10.2 us
    pallas_call x1, Pallas kernels, body(): pl.pallas_call(functools.partial(inverse_kernel, factors, dates), out_sha...  7.71 us
    all_to_all x2, starting transfers between devices, gather(): lax.all_to_all(jnp.broadcast_to(x, (lax.axis_size(axis), *x.shape)), axis...  7.07 us
    pallas_call x1, Pallas kernels, body(): pl.pallas_call(functools.partial(exposure_kernel, factors, dates), out_sh...  2.94 us
    broadcast_in_dim x2, local copies, waits for them, and re-layouts, gather(): jnp.broadcast_to(x, (lax.axis_size(axis), *x.shape))  1.83 us
  transfers between devices with their start and end apart: 4, of which 3 were waited for; matrix products, arithmetic and copies ran while one was open for 0% of the time, Pallas kernels for 9%

profile of v2, /device:TPU:0, one launch (start us, length us, event | category | flops | bytes accessed | tf_op | source)
XLA Modules:
  0.0 88.3 jit_solution(15024198545768843244)
XLA Ops:
  0.6 0.0 copy-start.2
  0.6 0.0 copy-start.1
  0.7 25.0 %net_moments.1 = f32[1024,128]{1,0:T(8,128)} custom-call(s32[4]{0:T(128)} %counts_ref.1, f32[32,512]{1,0:T(8,128)} %bitcast.14, f32[2,32,512]{2,1,0:T(8,128)} %bitcast.16, s32[1,512]{1,0:T(1,128)} %bitcast.18, f32[32,8192]{1,0:T(8,128)} %load_ref.1, f32[1,8192]{1,0:T(1,128)} %bitcast.20, f32[1,8192]{1,0:T(1,128)} %bitcast.21, s32[1,8192]{1,0:T(1,128)} %bitcast.22), custom_call_target="tpu_custom_call" | custom-call | flops 16000000000 | bytes 4000000 | tf_op jit(solution)/shard_map/net_moments/pallas_call | solution.py:234
  25.7 0.0 copy-start
  25.7 5.3 %all-to-all-start = ((f32[8,128,128]{2,1,0:T(8,128)}), f32[8,128,128]{2,1,0:T(8,128)S(1)}, u32[]{:S(2)}, u32[]{:S(2)}) async-start(f32[8,128,128]{2,1,0:T(8,128)} %bitcast.13), calls=%async_computation | async-start | bytes 1048576 | tf_op jit(solution)/shard_map/all_to_all | solution.py:192
  31.0 0.0 copy-done.2
  31.0 0.0 copy-done.1
  31.0 9.7 %all-to-all-done.parts_ref = f32[8,128,128]{2,1,0:T(8,128)S(1)} async-done(((f32[8,128,128]{2,1,0:T(8,128)}), f32[8,128,128]{2,1,0:T(8,128)S(1)}, u32[]{:S(2)}, u32[]{:S(2)}) %all-to-all-start) | async-done | bytes 524320 | tf_op jit(solution)/shard_map/all_to_all | solution.py:192
  40.8 0.7 add_parts.2
  41.4 4.9 %all-to-all-start.1 = ((f32[4,32,128]{2,1,0:T(8,128)}), f32[4,32,128]{2,1,0:T(8,128)S(1)}, u32[]{:S(2)}, u32[]{:S(2)}) async-start(f32[4,32,128]{2,1,0:T(8,128)} %bitcast.7), calls=%async_computation.1 | async-start | bytes 131072 | tf_op jit(solution)/shard_map/all_to_all | solution.py:192
  46.3 0.0 copy-done
  46.3 5.7 %all-to-all-done.1.parts_ref = f32[4,32,128]{2,1,0:T(8,128)S(1)} async-done(((f32[4,32,128]{2,1,0:T(8,128)}), f32[4,32,128]{2,1,0:T(8,128)S(1)}, u32[]{:S(2)}, u32[]{:S(2)}) %all-to-all-start.1) | async-done | bytes 65568 | tf_op jit(solution)/shard_map/all_to_all | solution.py:192
  52.0 1.2 %broadcast_in_dim.32 = f32[8,72,512]{2,1,0:T(8,128)} broadcast(f32[72,512]{1,0:T(8,128)S(1)} %pad_maximum_fusion.own_ref), dimensions={1,2} | broadcast | bytes 1327104 | tf_op jit(solution)/shard_map/broadcast_in_dim | solution.py:205
  53.2 0.0 copy-start.3
  53.2 3.7 %all-to-all-start.3 = ((f32[8,72,512]{2,1,0:T(8,128)}), f32[8,72,512]{2,1,0:T(8,128)S(1)}, u32[]{:S(2)}, u32[]{:S(2)}) async-start(f32[8,72,512]{2,1,0:T(8,128)} %broadcast_in_dim.32), calls=%async_computation.3 | async-start | bytes 2359296 | tf_op jit(solution)/shard_map/all_to_all | solution.py:205
  56.9 0.0 copy-done.3
  56.9 0.1 copy.11.limits_ref
  57.1 16.6 %all-to-all-done.3.blocks_ref = f32[8,72,512]{2,1,0:T(8,128)S(1)} async-done(((f32[8,72,512]{2,1,0:T(8,128)}), f32[8,72,512]{2,1,0:T(8,128)S(1)}, u32[]{:S(2)}, u32[]{:S(2)}) %all-to-all-start.3) | async-done | bytes 1179680 | tf_op jit(solution)/shard_map/all_to_all | solution.py:205
  73.6 0.7 broadcast_in_dim.30
  74.3 3.4 %all-to-all-start.2 = ((f32[8,32,128]{2,1,0:T(8,128)}), f32[8,32,128]{2,1,0:T(8,128)S(1)}, u32[]{:S(2)}, u32[]{:S(2)}) async-start(f32[8,32,128]{2,1,0:T(8,128)} %broadcast_in_dim.30), calls=%async_computation.2 | async-start | bytes 262144 | tf_op jit(solution)/shard_map/all_to_all | solution.py:205
  77.7 7.7 %gram_inverse.1.inverse_ref = f32[2,64,64]{2,1,0:T(8,128)S(1)} custom-call(f32[8,72,512]{2,1,0:T(8,128)S(1)} %all-to-all-done.3.blocks_ref), custom_call_target="tpu_custom_call" | custom-call | flops 8000000000 | bytes 1000000 | tf_op jit(solution)/shard_map/gram_inverse/pallas_call | solution.py:255
  85.4 0.0 all-to-all-done.2
  85.4 2.9 %set_exposure.1 = (f32[2,256,512]{2,1,0:T(8,128)}, f32[2,256]{1,0:T(2,128)}) custom-call(f32[256,128]{1,0:T(8,128)S(1)} %bitcast.12, f32[72,512]{1,0:T(8,128)S(1)} %pad_maximum_fusion.own_ref, f32[8,72,512]{2,1,0:T(8,128)S(1)} %all-to-all-done.3.blocks_ref, f32[2,64,64]{2,1,0:T(8,128)S(1)} %gram_inverse.1.inverse_ref, s32[256,1]{1,0:T(8,128)S(1)} %copy.11.limits_ref), custom_call_target="tpu_custom_call" | custom-call | flops 2000000000 | bytes 2000000 | tf_op jit(solution)/shard_map/set_exposure/pallas_call | solution.py:265
  (5 shorter events, 0.0 us)
Async XLA Ops:
  0.6 30.4 %copy-start.2 = (s32[512]{0:T(512)S(1)}, s32[512]{0:T(512)}, u32[]{:S(2)}) copy-start(s32[512]{0:T(512)} %param.16) | copy-start | bytes 6148
  0.6 30.4 %copy-start.1 = (f32[2,512,32]{1,2,0:T(8,128)S(1)}, f32[2,512,32]{1,2,0:T(8,128)}, u32[]{:S(2)}) copy-start(f32[2,512,32]{1,2,0:T(8,128)} %param.10) | copy-start | bytes 393220
  25.7 20.6 %copy-start = (f32[512,32]{0,1:T(8,128)S(1)}, f32[512,32]{0,1:T(8,128)}, u32[]{:S(2)}) copy-start(f32[512,32]{0,1:T(8,128)} %param.9) | copy-start | bytes 196612
  25.7 15.1 %all-to-all-start = ((f32[8,128,128]{2,1,0:T(8,128)}), f32[8,128,128]{2,1,0:T(8,128)S(1)}, u32[]{:S(2)}, u32[]{:S(2)}) async-start(f32[8,128,128]{2,1,0:T(8,128)} %bitcast.13), calls=%async_computation | async-start | bytes 1048576 | tf_op jit(solution)/shard_map/all_to_all | solution.py:192
  41.4 10.6 %all-to-all-start.1 = ((f32[4,32,128]{2,1,0:T(8,128)}), f32[4,32,128]{2,1,0:T(8,128)S(1)}, u32[]{:S(2)}, u32[]{:S(2)}) async-start(f32[4,32,128]{2,1,0:T(8,128)} %bitcast.7), calls=%async_computation.1 | async-start | bytes 131072 | tf_op jit(solution)/shard_map/all_to_all | solution.py:192
  53.2 3.7 %copy-start.3 = (s32[256]{0:T(256)S(1)}, s32[256]{0:T(256)}, u32[]{:S(2)}) copy-start(s32[256]{0:T(256)} %param.17) | copy-start | bytes 3076
  53.2 20.4 %all-to-all-start.3 = ((f32[8,72,512]{2,1,0:T(8,128)}), f32[8,72,512]{2,1,0:T(8,128)S(1)}, u32[]{:S(2)}, u32[]{:S(2)}) async-start(f32[8,72,512]{2,1,0:T(8,128)} %broadcast_in_dim.32), calls=%async_computation.3 | async-start | bytes 2359296 | tf_op jit(solution)/shard_map/all_to_all | solution.py:205
  74.3 11.1 %all-to-all-start.2 = ((f32[8,32,128]{2,1,0:T(8,128)}), f32[8,32,128]{2,1,0:T(8,128)S(1)}, u32[]{:S(2)}, u32[]{:S(2)}) async-start(f32[8,32,128]{2,1,0:T(8,128)} %broadcast_in_dim.30), calls=%async_computation.2 | async-start | bytes 262144 | tf_op jit(solution)/shard_map/all_to_all | solution.py:205
